TPU v7x, 32 devices: a whole 2x2x4 slice. The times are simulated.
32 devices in a mesh: seq: 8 (over z, x), head: 4 (over y, core).
Axes of the slice: x: 2, y: 2, z: 4, core: 2. Of those that a mesh axis runs over, the one named last changes fastest.
Arguments:
- hidden_in: bfloat16 [1024, 2048], P('seq', 'head'), may hold values from -6 to 6
- out_grad: float32 [1024, 2048], P('seq', 'head'), may hold values from -6 to 6
- expert_ids: int32 [1024, 8], P('seq'), may hold values from 0 to 63, all different within a row; in each aligned block of 128 rows (0 to 127, 128 to 255, ...) at most 32 rows name the same one
- route_weights: float32 [1024, 8], P('seq'), may hold values from 0.03 to 0.3
- w_gate: bfloat16 [64, 2048, 1024], P('seq', None, 'head'), may hold values from -0.125 to 0.125
- w_up: bfloat16 [64, 2048, 1024], P('seq', None, 'head'), may hold values from -0.125 to 0.125
- w_down: bfloat16 [64, 1024, 2048], P('seq', 'head'), may hold values from -0.1875 to 0.1875
- query_in: float32 [1024, 2048], P('seq', 'head'), may hold values from -6 to 6
- key_in: float32 [1024, 2048], P('seq', 'head'), may hold values from -6 to 6
- value_in: float32 [1024, 2048], P('seq', 'head'), may hold values from -6 to 6
- state_before: float32 [16, 128, 128], P('head'), may hold values from -192 to 192
- grad_after: float32 [16, 128, 128], P('head'), may hold values from -192 to 192
Outputs:
- grad_gate: bfloat16 [64, 2048, 1024], P('seq', None, 'head')
- grad_up: bfloat16 [64, 2048, 1024], P('seq', None, 'head')
- grad_down: bfloat16 [64, 1024, 2048], P('seq', 'head')
- grad_query: float32 [1024, 2048], P('seq', 'head')
- grad_key: float32 [1024, 2048], P('seq', 'head')
- grad_value: float32 [1024, 2048], P('seq', 'head')
Inputs may be any that keep to these rules, and one draw needn't show every extreme that they name: `expert_ids`: each row names 8 different experts. Among the 128 rows of one index of seq (aligned blocks of 128 rows) no expert is named more than 32 times, a bound that some block reaches.
All inputs are finite; a program needn't handle non-finite values.
Results may differ from a plain program's by a relative error of at most 0.014.
Values may be sent and summed in bfloat16 or wider, within the bound.
A program may use at most 128 MiB of HBM per device.

v0:
```python
import jax
import jax.numpy as jnp
from jax import lax
from jax.sharding import PartitionSpec as P

EXPERTS = 64
TOPK = 8
HD = 128
CAP = 32


HIGHEST = lax.Precision.HIGHEST


def carried_in(shard, axis, join, neutral, backward):
    count = lax.axis_size(axis)
    place = lax.axis_index(axis)
    ahead = count - 1 - place if backward else place
    gathered = lax.all_gather(shard.astype(jnp.bfloat16), axis)
    state = jnp.zeros_like(shard) + jnp.asarray(neutral, shard.dtype)

    def one(turn, state):
        source = count - 1 - turn if backward else turn
        return join(state, lax.dynamic_index_in_dim(gathered, source, 0, False).astype(shard.dtype))

    return lax.fori_loop(0, ahead, one, state)


def add_states(earlier, later):
    return earlier + later


def attention_backward(query_in, key_in, value_in, attn_grad, prefix, suffix, attn_scale):
    block_len = query_in.shape[0]
    causal = jnp.arange(block_len)[:, None] >= jnp.arange(block_len)[None, :]
    score_grad = jnp.einsum("thj,shj->hts", attn_grad, value_in, precision=HIGHEST)
    score_grad = jnp.where(causal[None], score_grad, 0.0)
    score_match = jnp.einsum("thi,shi->hts", query_in, key_in, precision=HIGHEST)
    score_match = jnp.where(causal[None], score_match, 0.0)
    grad_query = jnp.einsum("hts,shi->thi", score_grad, key_in, precision=HIGHEST)
    grad_query = grad_query + jnp.einsum("thj,hij->thi", attn_grad, prefix, precision=HIGHEST)
    grad_key = jnp.einsum("hts,thi->shi", score_grad, query_in, precision=HIGHEST)
    grad_key = grad_key + jnp.einsum("shj,hij->shi", value_in, suffix, precision=HIGHEST)
    grad_value = jnp.einsum("hts,thj->shj", score_match, attn_grad, precision=HIGHEST)
    grad_value = grad_value + jnp.einsum("shi,hij->shj", key_in, suffix, precision=HIGHEST)
    return (grad_query * attn_scale, grad_key * attn_scale, grad_value * attn_scale)


def expert_backward(row_data, grad_rows, w_gate, w_up, w_down):
    pre_gate = jnp.einsum("erd,edf->erf", row_data, w_gate, preferred_element_type=jnp.float32)
    pre_up = jnp.einsum("erd,edf->erf", row_data, w_up, preferred_element_type=jnp.float32)
    gate_sigmoid = jax.nn.sigmoid(pre_gate)
    gate_swish = pre_gate * gate_sigmoid
    hidden_act = (gate_swish * pre_up).astype(jnp.bfloat16)
    d_inner = jnp.einsum("erd,efd->erf", grad_rows, w_down, preferred_element_type=jnp.float32)
    d_gate = (d_inner * pre_up * gate_sigmoid * (1.0 + pre_gate * (1.0 - gate_sigmoid))).astype(
        jnp.bfloat16
    )
    d_up = (d_inner * gate_swish).astype(jnp.bfloat16)
    grad_down = jnp.einsum(
        "erf,erd->efd", hidden_act, grad_rows, preferred_element_type=jnp.float32
    )
    grad_gate = jnp.einsum("erd,erf->edf", row_data, d_gate, preferred_element_type=jnp.float32)
    grad_up = jnp.einsum("erd,erf->edf", row_data, d_up, preferred_element_type=jnp.float32)
    hidden_part = jnp.einsum("erf,edf->erd", d_gate, w_gate, preferred_element_type=jnp.float32)
    hidden_part = hidden_part + jnp.einsum(
        "erf,edf->erd", d_up, w_up, preferred_element_type=jnp.float32
    )
    return (
        grad_gate.astype(jnp.bfloat16),
        grad_up.astype(jnp.bfloat16),
        grad_down.astype(jnp.bfloat16),
        hidden_part,
    )


def per_device(
    hidden_in,
    out_grad,
    expert_ids,
    route_weights,
    w_gate,
    w_up,
    w_down,
    query_in,
    key_in,
    value_in,
    state_before,
    grad_after,
):
    seq_count = lax.axis_size("seq")
    tok_rows = expert_ids.shape[0]
    exp_local = w_gate.shape[0]
    slot_count = exp_local * seq_count * CAP
    head_local = query_in.shape[1] // HD
    query_heads = query_in.reshape(tok_rows, head_local, HD)
    key_heads = key_in.reshape(tok_rows, head_local, HD)
    value_heads = value_in.reshape(tok_rows, head_local, HD)
    kv_local = jnp.einsum("shi,shj->hij", key_heads, value_heads, precision=HIGHEST)
    prefix = carried_in(kv_local, "seq", add_states, jnp.zeros_like(kv_local), False)
    prefix = prefix + state_before
    flat_ids = expert_ids.reshape(-1)
    onehot = (flat_ids[:, None] == jnp.arange(EXPERTS, dtype=jnp.int32)[None, :]).astype(jnp.int32)
    slot_rank = jnp.sum((jnp.cumsum(onehot, axis=0) - onehot) * onehot, axis=1)
    slot_dest = (flat_ids % exp_local * seq_count + flat_ids // exp_local) * CAP + slot_rank
    feat_width = hidden_in.shape[1]
    pair_rows = jnp.broadcast_to(hidden_in[:, None, :], (tok_rows, TOPK, feat_width)).reshape(
        -1, feat_width
    )
    pair_grad = (
        (route_weights[:, :, None] * out_grad[:, None, :])
        .astype(jnp.bfloat16)
        .reshape(-1, feat_width)
    )
    send_rows = jnp.zeros((slot_count, feat_width), jnp.bfloat16).at[slot_dest].set(pair_rows)
    send_rows = send_rows.reshape(exp_local, seq_count, CAP, feat_width)
    send_grad = jnp.zeros((slot_count, feat_width), jnp.bfloat16).at[slot_dest].set(pair_grad)
    send_grad = send_grad.reshape(exp_local, seq_count, CAP, feat_width)
    quarter_rows, quarter_grad = (
        lax.all_to_all(send_rows, "seq", split_axis=1, concat_axis=1, tiled=True),
        lax.all_to_all(send_grad, "seq", split_axis=1, concat_axis=1, tiled=True),
    )
    expert_rows, expert_grad = (
        lax.all_gather(quarter_rows, "head", axis=3, tiled=True),
        lax.all_gather(quarter_grad, "head", axis=3, tiled=True),
    )
    model_width = expert_rows.shape[3]
    row_data = expert_rows.reshape(exp_local, seq_count * CAP, model_width)
    grad_rows = expert_grad.reshape(exp_local, seq_count * CAP, model_width)
    grad_gate, grad_up, grad_down, hidden_part = expert_backward(
        row_data, grad_rows, w_gate, w_up, w_down
    )
    hidden_part = hidden_part.reshape(exp_local, seq_count, CAP, model_width)
    returned = lax.all_to_all(
        hidden_part.astype(jnp.bfloat16), "seq", split_axis=1, concat_axis=1, tiled=True
    )
    token_part = returned.reshape(-1, model_width)[slot_dest].astype(jnp.float32)
    token_part = token_part.reshape(tok_rows, TOPK, model_width).sum(axis=1)
    moe_grad = lax.psum_scatter(
        token_part.astype(jnp.bfloat16), "head", scatter_dimension=1, tiled=True
    ).astype(jnp.float32)
    attn_grad = (out_grad + moe_grad).reshape(tok_rows, head_local, HD)
    qd_local = jnp.einsum("thi,thj->hij", query_heads, attn_grad, precision=HIGHEST)
    suffix = carried_in(qd_local, "seq", add_states, jnp.zeros_like(qd_local), True)
    suffix = suffix + grad_after
    attn_scale = (HD * tok_rows * seq_count) ** (-0.5)
    grad_query, grad_key, grad_value = attention_backward(
        query_heads, key_heads, value_heads, attn_grad, prefix, suffix, attn_scale
    )
    return (
        grad_gate,
        grad_up,
        grad_down,
        grad_query.reshape(tok_rows, -1),
        grad_key.reshape(tok_rows, -1),
        grad_value.reshape(tok_rows, -1),
    )


def solution(mesh):
    placed = (
        P("seq", "head"),
        P("seq", "head"),
        P("seq", None),
        P("seq", None),
        P("seq", None, "head"),
        P("seq", None, "head"),
        P("seq", "head", None),
        P("seq", "head"),
        P("seq", "head"),
        P("seq", "head"),
        P("head", None, None),
        P("head", None, None),
    )
    return jax.shard_map(
        per_device,
        mesh=mesh,
        in_specs=placed,
        out_specs=(
            P("seq", None, "head"),
            P("seq", None, "head"),
            P("seq", "head", None),
            P("seq", "head"),
            P("seq", "head"),
            P("seq", "head"),
        ),
        check_vma=False,
    )
```

profile of v0, /device:TPU:0, one launch (start us, length us, event | category | flops | bytes accessed | tf_op | source)
XLA Modules:
  0.0 568.9 jit_solution(14966094470612000109)
XLA Ops:
  9.2 18.0 %reduce-window.6 = s32[64,8,128]{2,1,0:T(8,128)S(1)} reduce-window(s32[64,8,128]{2,1,0:T(8,128)S(1)} %fusion.32, s32[]{:T(128)} %constant.75.clone.1), window={size=1x1x128 pad=0_0x0_0x127_0}, to_apply=%region_0.1 | reduce-window | flops 8323072 | bytes 524292 | tf_op jit(solution)/shard_map/reduce-window
  27.9 6.1 %scatter_custom_fusion = bf16[2048,512]{1,0:T(8,128)(2,1)S(1)} fusion(s32[1024]{0:T(1024)S(1)} %bitcast.174, bf16[]{:T(256)} %constant.74.clone.1, bf16[128,512]{1,0:T(8,128)(2,1)} %param.16), kind=kCustom, calls=%fused_computation.33 | custom fusion | bytes 2228226 | tf_op jit(solution)/shard_map/scatter | solution.py:115
  34.2 55.4 %all_to_all.15 = bf16[8,8,32,512]{3,2,0,1:T(8,128)(2,1)} all-to-all(bf16[8,8,32,512]{3,2,0,1:T(8,128)(2,1)S(1)} %copy.101), channel_id=1, replica_groups=mesh['seq'=8,'head'=4] {'seq'}, dimensions={1} | all-to-all | bytes 4194304 | tf_op jit(solution)/shard_map/all_to_all | solution.py:120
  89.9 6.2 %scatter_custom_fusion.1 = bf16[2048,512]{1,0:T(8,128)(2,1)S(1)} fusion(s32[1024]{0:T(1024)S(1)} %bitcast.175, f32[128,512]{1,0:T(8,128)S(1)} %copy-done.5, f32[1024]{0:T(1024)S(1)} %mul.82, bf16[]{:T(256)} %constant.74.clone.1), kind=kCustom, calls=%fused_computation.32 | custom fusion | flops 1048576 | bytes 2363394 | tf_op jit(solution)/shard_map/scatter | solution.py:117
  96.4 51.6 %all_to_all.16 = bf16[8,8,32,512]{3,2,0,1:T(8,128)(2,1)} all-to-all(bf16[8,8,32,512]{3,2,0,1:T(8,128)(2,1)S(1)} %copy.104), channel_id=1, replica_groups=mesh['seq'=8,'head'=4] {'seq'}, dimensions={1} | all-to-all | bytes 4194304 | tf_op jit(solution)/shard_map/all_to_all | solution.py:121
  148.1 9.1 %copy.102 = bf16[8,8,32,2048]{3,2,1,0:T(8,128)(2,1)} copy(bf16[8,8,32,2048]{3,2,0,1:T(8,128)(2,1)} %all-gather.7.cloned.1.call-done) | data formatting | bytes 16777216 | tf_op jit(solution)/shard_map/all_gather | solution.py:124
  157.2 11.2 %fusion.48 = f32[8,256,256]{2,1,0:T(8,128)} fusion(bf16[8,256,2048]{2,1,0:T(8,128)(2,1)} %bitcast.151, bf16[8,2048,256]{2,1,0:T(8,128)(2,1)} %param.21), kind=kOutput, calls=%fused_computation.83 | convolution fusion | flops 2147483648 | bytes 18874368 | tf_op jit(solution)/shard_map/erd,edf->erf/dot_general | solution.py:51
  169.0 3.9 fusion.49
  172.8 34.2 %all-gather.9.cloned.1.call-done = bf16[8,8,32,2048]{3,2,0,1:T(8,128)(2,1)} async-done(((bf16[8,8,32,512]{3,2,0,1:T(8,128)(2,1)}), bf16[8,8,32,2048]{3,2,0,1:T(8,128)(2,1)}) %all-gather.9.cloned.1.call-update) | async-done | bytes 8388624 | tf_op jit(solution)/shard_map/all_gather | solution.py:125
  207.0 8.4 %copy.105 = bf16[8,8,32,2048]{3,2,1,0:T(8,128)(2,1)} copy(bf16[8,8,32,2048]{3,2,0,1:T(8,128)(2,1)} %all-gather.9.cloned.1.call-done) | data formatting | bytes 16777216 | tf_op jit(solution)/shard_map/all_gather | solution.py:125
  215.5 10.0 %multiply_convert_fusion.1 = (bf16[8,256,256]{2,1,0:T(8,128)(2,1)S(1)}, bf16[8,256,256]{2,1,0:T(8,128)(2,1)S(1)}) fusion(f32[8,256,256]{2,1,0:T(8,128)} %fusion.49, f32[8,256,256]{2,1,0:T(8,128)} %fusion.48, bf16[8,256,2048]{2,1,0:T(8,128)(2,1)} %bitcast.155, bf16[8,256,2048]{2,1,0:T(8,128)(2,1)} %param.22), kind=kOutput, calls=%fused_computation.13 | convolution fusion | flops 2154299392 | bytes 23068672 | tf_op jit(solution)/shard_map/erd,efd->erf/dot_general | solution.py:55
  225.5 11.5 %fusion.50 = f32[8,256,2048]{2,1,0:T(8,128)} fusion(bf16[8,256,256]{2,1,0:T(8,128)(2,1)S(1)} %get-tuple-element.136, bf16[8,2048,256]{2,1,0:T(8,128)(2,1)} %param.20), kind=kOutput, calls=%fused_computation.85 | convolution fusion | flops 2147483648 | bytes 26214400 | tf_op jit(solution)/shard_map/erf,edf->erd/dot_general | solution.py:65
  237.0 13.7 %add_convert_fusion = bf16[8,256,2048]{2,1,0:T(8,128)(2,1)} fusion(f32[8,256,2048]{2,1,0:T(8,128)} %fusion.50, bf16[8,256,256]{2,1,0:T(8,128)(2,1)S(1)} %get-tuple-element.135, bf16[8,2048,256]{2,1,0:T(8,128)(2,1)} %param.21), kind=kOutput, calls=%fused_computation.5 | convolution fusion | flops 2155872256 | bytes 34603008 | tf_op jit(solution)/shard_map/erf,edf->erd/dot_general | solution.py:66
  250.8 8.4 %copy.109 = bf16[8,8,32,2048]{3,2,0,1:T(8,128)(2,1)} copy(bf16[8,8,32,2048]{3,2,1,0:T(8,128)(2,1)} %bitcast.157) | data formatting | bytes 16777216 | tf_op jit(solution)/shard_map/convert_element_type | solution.py:135
  259.2 5.6 all-to-all-start.2
  264.9 1.3 convolution_convert_fusion.4
  267.0 194.7 %all-gather.11.cloned.1.call-done = bf16[32,128,128]{2,1,0:T(8,128)(2,1)} async-done(((bf16[4,128,128]{2,1,0:T(8,128)(2,1)}), bf16[32,128,128]{2,1,0:T(8,128)(2,1)}) %all-gather.11.cloned.1.call-update) | async-done | bytes 1048592 | tf_op jit(solution)/shard_map/all_gather | solution.py:19
  461.7 8.4 %copy.110 = bf16[8,8,32,2048]{3,2,1,0:T(8,128)(2,1)} copy(bf16[8,8,32,2048]{3,2,0,1:T(8,128)(2,1)} %all-to-all-done.2) | data formatting | bytes 16777216 | tf_op jit(solution)/shard_map/all_to_all | solution.py:134
  470.2 13.3 %gather_fusion = bf16[1024,2048]{1,0:T(8,128)(2,1)} fusion(bf16[2048,2048]{1,0:T(8,128)(2,1)} %bitcast.150, s32[1024]{0:T(1024)S(1)} %broadcast_clamp_fusion), kind=kCustom, calls=%fused_computation | custom fusion | bytes 8392704 | tf_op jit(solution)/shard_map/gather | solution.py:137
  483.4 5.9 %bitcast_reduce_fusion = bf16[128,2048]{1,0:T(8,128)(2,1)} fusion(bf16[1024,2048]{1,0:T(8,128)(2,1)} %gather_fusion), kind=kLoop, calls=%fused_computation.9 | loop fusion | flops 1835008 | bytes 4718592 | tf_op jit(solution)/shard_map/reduce_sum | solution.py:138
  489.6 9.6 %convolution_convert_fusion.1 = bf16[8,2048,256]{2,1,0:T(8,128)(2,1)} fusion(bf16[8,256,2048]{2,1,0:T(8,128)(2,1)} %bitcast.152, bf16[8,256,256]{2,1,0:T(8,128)(2,1)S(1)} %get-tuple-element.135), kind=kOutput, calls=%fused_computation.7 | convolution fusion | flops 2151677952 | bytes 17825792 | tf_op jit(solution)/shard_map/erd,erf->edf/dot_general | solution.py:64
  499.3 10.6 %convolution_convert_fusion = bf16[8,256,2048]{2,1,0:T(8,128)(2,1)} fusion(bf16[8,256,2048]{2,1,0:T(8,128)(2,1)} %bitcast.156, f32[8,256,256]{2,1,0:T(8,128)} %fusion.48, f32[8,256,256]{2,1,0:T(8,128)} %fusion.49), kind=kOutput, calls=%fused_computation.6 | convolution fusion | flops 2154823680 | bytes 20971520 | tf_op jit(solution)/shard_map/erf,erd->efd/dot_general | solution.py:60
  512.2 9.6 %convolution_convert_fusion.2 = bf16[8,2048,256]{2,1,0:T(8,128)(2,1)} fusion(bf16[8,256,2048]{2,1,0:T(8,128)(2,1)} %bitcast.153, bf16[8,256,256]{2,1,0:T(8,128)(2,1)S(1)} %get-tuple-element.136), kind=kOutput, calls=%fused_computation.8 | convolution fusion | flops 2151677952 | bytes 17825792 | tf_op jit(solution)/shard_map/erd,erf->edf/dot_general | solution.py:63
  525.2 26.2 %all-gather.13.cloned.1.call-done = bf16[32,128,128]{2,1,0:T(8,128)(2,1)} async-done(((bf16[4,128,128]{2,1,0:T(8,128)(2,1)}), bf16[32,128,128]{2,1,0:T(8,128)(2,1)}) %all-gather.13.cloned.1.call-update) | async-done | bytes 1048592 | tf_op jit(solution)/shard_map/all_gather | solution.py:19
  551.4 6.9 %while.23 = (s32[]{:T(128)}, f32[4,128,128]{2,1,0:T(8,128)S(1)}, s32[]{:T(128)}, bf16[8,4,128,128]{3,2,1,0:T(8,128)(2,1)}, s32[]{:T(128)}, /*index=5*/s32[]{:T(128)}, s32[]{:T(128)}, s32[]{:T(128)}) while((s32[]{:T(128)}, f32[4,128,128]{2,1,0:T(8,128)S(1)}, s32[]{:T(128)}, bf16[8,4,128,128]{3,2,1,0:T(8,128)(2,1)}, s32[]{:T(128)}, ...), condition=%wide.region_10.11_spmd, body=%wide.region_9.10_spmd.sunk | while | flops 131078 | bytes 655495 | solution.py:26
  551.5 1.0 convert_add_fusion.6
  552.5 1.0 convert_add_fusion.6
  553.4 1.0 convert_add_fusion.6
  554.4 1.0 convert_add_fusion.6
  555.4 1.0 convert_add_fusion.6
  556.4 1.0 convert_add_fusion.6
  557.4 1.0 convert_add_fusion.6
  (73 shorter events, 13.0 us)
Async XLA Ops:
  8.0 256.9 %copy-start = (f32[128,512]{1,0:T(8,128)S(1)}, f32[128,512]{1,0:T(8,128)}, u32[]{:S(2)}) copy-start(f32[128,512]{1,0:T(8,128)} %param.24) | copy-start | bytes 786436
  8.0 81.7 %copy-start.8 = (f32[128,8]{0,1:T(8,128)S(1)}, f32[128,8]{0,1:T(8,128)}, u32[]{:S(2)}) copy-start(f32[128,8]{0,1:T(8,128)} %param.19) | copy-start | bytes 12292
  8.0 81.9 %copy-start.5 = (f32[128,512]{1,0:T(8,128)S(1)}, f32[128,512]{1,0:T(8,128)}, u32[]{:S(2)}) copy-start(f32[128,512]{1,0:T(8,128)} %param.17) | copy-start | bytes 786436
  8.0 140.0 %all-gather.7.cloned.1.call-start = ((), (), s32[]{:S(2)}) async-start(), calls=%async_computation.4 | async-start | bytes 10485760 | tf_op jit(solution)/shard_map/all_gather | solution.py:124
  89.7 117.4 %all-gather.9.cloned.1.call-start = ((), (), s32[]{:S(2)}) async-start(), calls=%async_computation.5 | async-start | bytes 10485760 | tf_op jit(solution)/shard_map/all_gather | solution.py:125
  148.0 20.3 %slice-start = ((s8[8388608]{0:T(1024)(128)(4,1)}), s8[4194304]{0:T(1024)(128)(4,1)S(1)}, s32[]{:S(2)}) async-start(s8[8388608]{0:T(1024)(128)(4,1)} %bitcast.158), calls=%async_computation.9 | async-start | bytes 8388608
  157.2 11.2 %copy-start.1 = (bf16[8,8,32,2048]{3,2,1,0:T(8,128)(2,1)S(1)}, bf16[8,8,32,2048]{3,2,1,0:T(8,128)(2,1)}, u32[]{:S(2)}) copy-start(bf16[8,8,32,2048]{3,2,1,0:T(8,128)(2,1)} %copy.102) | copy-start | bytes 25165828
  157.2 11.8 %slice-start.1 = ((s8[8388608]{0:T(1024)(128)(4,1)}), s8[4194304]{0:T(1024)(128)(4,1)S(1)}, s32[]{:S(2)}) async-start(s8[8388608]{0:T(1024)(128)(4,1)} %bitcast.158), calls=%async_computation.10 | async-start | bytes 8388608
  259.2 5.7 %copy-start.3 = (f32[128,512]{1,0:T(8,128)S(1)}, f32[128,512]{1,0:T(8,128)}, u32[]{:S(2)}) copy-start(f32[128,512]{1,0:T(8,128)} %param.25) | copy-start | bytes 786436
  259.2 7.1 %copy-start.2 = (f32[128,512]{1,0:T(8,128)S(1)}, f32[128,512]{1,0:T(8,128)}, u32[]{:S(2)}) copy-start(f32[128,512]{1,0:T(8,128)} %param.23) | copy-start | bytes 786436
  259.2 202.5 %all-to-all-start.2 = ((bf16[8,8,32,2048]{3,2,0,1:T(8,128)(2,1)}), bf16[8,8,32,2048]{3,2,0,1:T(8,128)(2,1)}, u32[]{:S(2)}, u32[]{:S(2)}) async-start(bf16[8,8,32,2048]{3,2,0,1:T(8,128)(2,1)} %copy.109), calls=%async_computation.2 | async-start | bytes 16777216 | tf_op jit(solution)/shard_map/all_to_all | solution.py:134
  264.9 196.8 %all-gather.11.cloned.1.call-start = ((), (), s32[]{:S(2)}) async-start(), calls=%async_computation.7 | async-start | bytes 1179648 | tf_op jit(solution)/shard_map/all_gather | solution.py:19
  266.2 243.7 %reduce-scatter.2.cloned.1.call-start = ((), (), s32[]{:S(2)}) async-start(), calls=%async_computation.6 | async-start | bytes 655360 | tf_op jit(solution)/shard_map/reduce_scatter | solution.py:139
  489.3 62.1 %all-gather.13.cloned.1.call-start = ((), (), s32[]{:S(2)}) async-start(), calls=%async_computation.8 | async-start | bytes 1179648 | tf_op jit(solution)/shard_map/all_gather | solution.py:19
  499.3 10.6 %copy-start.6 = (f32[128,512]{1,0:T(8,128)S(1)}, f32[128,512]{1,0:T(8,128)}, u32[]{:S(2)}) copy-start(f32[128,512]{1,0:T(8,128)} %param.17) | copy-start | bytes 786436
  512.2 10.8 %copy-start.7 = (f32[4,128,128]{2,1,0:T(8,128)S(1)}, f32[4,128,128]{2,1,0:T(8,128)}, u32[]{:S(2)}) copy-start(f32[4,128,128]{2,1,0:T(8,128)} %param.26) | copy-start | bytes 786436
  521.8 36.6 %copy-start.4 = (f32[4,128,128]{2,1,0:T(8,128)S(1)}, f32[4,128,128]{2,1,0:T(8,128)}, u32[]{:S(2)}) copy-start(f32[4,128,128]{2,1,0:T(8,128)} %param.27) | copy-start | bytes 786436
Sparse Core Ops, SparseCore 0:
  89.8 57.3 all-gather.6
  148.7 58.2 all-gather.8
  489.5 19.1 reduce-scatter.1
Sparse Core Ops, SparseCore 1:
  268.3 193.4 all-gather.10
  512.3 39.1 all-gather.12
where the time goes:
time: 576 us; the launch traced here: 569 us
  waiting for transfers between devices  255 us (44%)
  blocking collectives  107 us (19%)
  matrix products  86.4 us (15%)
  local copies, waits for them, and re-layouts  60 us (10%)
  other arithmetic  38.1 us (7%)
  between operations  16 us (3%)
  starting transfers between devices  6.1 us (1%)
    all_gather x2, waiting for transfers between devices, carried_in(): gathered = lax.all_gather(shard.astype(jnp.bfloat16), axis)  221 us
    all_to_all x1, blocking collectives, per_device(): lax.all_to_all(send_rows, 'seq', split_axis=1, concat_axis=1, tiled=True)  55.4 us
    all_to_all x1, blocking collectives, per_device(): lax.all_to_all(send_grad, 'seq', split_axis=1, concat_axis=1, tiled=True)  51.6 us
    all_gather x1, waiting for transfers between devices, per_device(): lax.all_gather(quarter_grad, 'head', axis=3, tiled=True)  34.2 us
    another operation x3, other arithmetic  18.2 us
    dot_general x1, matrix products, expert_backward(): jnp.einsum('erf,edf->erd', d_up, w_up, preferred_element_type=jnp.float32)  13.7 us
    gather x1, local copies, waits for them, and re-layouts, per_device(): returned.reshape(-1, model_width)[slot_dest].astype(jnp.float32)  13.3 us
  transfers between devices with their start and end apart: 6, of which 3 were waited for; matrix products, arithmetic and copies ran while one was open for 12% of the time, Pallas kernels for 0%

commit v1 on v0

v1 whole, which is shorter than its diff:
```python
import jax
import jax.numpy as jnp
from jax import lax
from jax.experimental import pallas as pl
from jax.experimental.pallas import tpu as pltpu
from jax.sharding import PartitionSpec as P

EXPERTS = 64
TOPK = 8
HD = 128
CAP = 32


HIGHEST = lax.Precision.HIGHEST


def carried_in(shard, axis, backward):
    place = lax.axis_index(axis)
    gathered = lax.all_gather(shard.astype(jnp.bfloat16), axis).astype(jnp.float32)
    order = jnp.arange(gathered.shape[0])
    used = (order > place) if backward else (order < place)
    return jnp.sum(jnp.where(used[:, None, None, None], gathered, 0.0), axis=0)


def attention_backward(query_in, key_in, value_in, attn_grad, prefix, suffix, attn_scale):
    block_len = query_in.shape[0]
    causal = jnp.arange(block_len)[:, None] >= jnp.arange(block_len)[None, :]
    score_grad = jnp.einsum("thj,shj->hts", attn_grad, value_in, precision=HIGHEST)
    score_grad = jnp.where(causal[None], score_grad, 0.0)
    score_match = jnp.einsum("thi,shi->hts", query_in, key_in, precision=HIGHEST)
    score_match = jnp.where(causal[None], score_match, 0.0)
    grad_query = jnp.einsum("hts,shi->thi", score_grad, key_in, precision=HIGHEST)
    grad_query = grad_query + jnp.einsum("thj,hij->thi", attn_grad, prefix, precision=HIGHEST)
    grad_key = jnp.einsum("hts,thi->shi", score_grad, query_in, precision=HIGHEST)
    grad_key = grad_key + jnp.einsum("shj,hij->shi", value_in, suffix, precision=HIGHEST)
    grad_value = jnp.einsum("hts,thj->shj", score_match, attn_grad, precision=HIGHEST)
    grad_value = grad_value + jnp.einsum("shi,hij->shj", key_in, suffix, precision=HIGHEST)
    return (grad_query * attn_scale, grad_key * attn_scale, grad_value * attn_scale)


NT = (((1,), (1,)), ((), ()))
TN = (((0,), (0,)), ((), ()))


def dot(a, b, dims=(((1,), (0,)), ((), ()))):
    return lax.dot_general(a, b, dims, preferred_element_type=jnp.float32)


def expert_kernel(
    seq_count,
    exp_local,
    x_ref,
    wg_ref,
    wu_ref,
    wd_ref,
    gg_ref,
    gu_ref,
    gd_ref,
    part_ref,
    rows,
    grads,
    picks,
    route,
):
    step = pl.program_id(0)
    heads, tok_rows, _ = x_ref.shape
    feat = part_ref.shape[3]

    @pl.when(step < seq_count)
    def _gather():
        base = lax.axis_index("seq") * exp_local
        route[...] = x_ref[0, :, 2 * feat :].astype(jnp.float32)
        ranks = lax.broadcasted_iota(jnp.int32, (CAP, tok_rows), 0).astype(jnp.float32)
        ones, scaled = [], []
        for e in range(exp_local):
            rank_row = route[pl.ds(base + e, 1), :]
            weight_row = route[pl.ds(EXPERTS + base + e, 1), :]
            hit = ranks == rank_row
            ones.append(jnp.where(hit, 1.0, 0.0))
            scaled.append(jnp.where(hit, weight_row, 0.0))
        one = jnp.concatenate(ones, axis=0).astype(jnp.bfloat16)
        weighted = jnp.concatenate(scaled, axis=0).astype(jnp.bfloat16)
        picks[step] = one
        at = pl.ds(pl.multiple_of(step * CAP, CAP), CAP)
        for h in range(heads):
            cols = pl.ds(h * feat, feat)
            got = dot(one, x_ref[h, :, :feat]).astype(jnp.bfloat16)
            rows[:, at, cols] = got.reshape(exp_local, CAP, feat)
            got = dot(weighted, x_ref[h, :, feat : 2 * feat]).astype(jnp.bfloat16)
            grads[:, at, cols] = got.reshape(exp_local, CAP, feat)

    @pl.when((step >= seq_count) & (step < seq_count + exp_local))
    def _expert():
        e = step - seq_count
        xr = rows[e]
        gr = grads[e]
        wg = wg_ref[0]
        wu = wu_ref[0]
        pre_gate = dot(xr, wg)
        pre_up = dot(xr, wu)
        d_inner = dot(gr, wd_ref[0], NT)
        sig = jax.nn.sigmoid(pre_gate)
        swish = pre_gate * sig
        act = (swish * pre_up).astype(jnp.bfloat16)
        d_gate = (d_inner * pre_up * sig * (1.0 + pre_gate * (1.0 - sig))).astype(jnp.bfloat16)
        d_up = (d_inner * swish).astype(jnp.bfloat16)
        gd_ref[0] = dot(act, gr, TN).astype(jnp.bfloat16)
        gg_ref[0] = dot(xr, d_gate, TN).astype(jnp.bfloat16)
        gu_ref[0] = dot(xr, d_up, TN).astype(jnp.bfloat16)
        rows[e] = (dot(d_gate, wg, NT) + dot(d_up, wu, NT)).astype(jnp.bfloat16)

    @pl.when(step >= seq_count + exp_local)
    def _combine():
        b = step - seq_count - exp_local
        at = pl.ds(pl.multiple_of(b * CAP, CAP), CAP)
        for h in range(heads):
            back = rows[:, at, pl.ds(h * feat, feat)].reshape(exp_local * CAP, feat)
            part_ref[0, h] = dot(picks[b], back, TN).astype(jnp.bfloat16)


def expert_call(x_all, w_gate, w_up, w_down):
    seq_count, heads, tok_rows, width = x_all.shape
    exp_local, model, hidden = w_gate.shape
    feat = model // heads
    slots = seq_count * CAP

    def expert_at(i):
        return (jnp.clip(i - seq_count, 0, exp_local - 1), 0, 0)

    def block_in(i):
        return (jnp.minimum(i, seq_count - 1), 0, 0, 0)

    def block_out(i):
        return (jnp.maximum(i - seq_count - exp_local, 0), 0, 0, 0)

    tall = pl.BlockSpec((1, model, hidden), expert_at)
    flat = pl.BlockSpec((1, hidden, model), expert_at)
    return pl.pallas_call(
        lambda *refs: expert_kernel(seq_count, exp_local, *refs),
        grid=(2 * seq_count + exp_local,),
        in_specs=[pl.BlockSpec((None, heads, tok_rows, width), block_in), tall, tall, flat],
        out_specs=[tall, tall, flat, pl.BlockSpec((1, heads, tok_rows, feat), block_out)],
        out_shape=[
            jax.ShapeDtypeStruct(w_gate.shape, jnp.bfloat16),
            jax.ShapeDtypeStruct(w_up.shape, jnp.bfloat16),
            jax.ShapeDtypeStruct(w_down.shape, jnp.bfloat16),
            jax.ShapeDtypeStruct((seq_count, heads, tok_rows, feat), jnp.bfloat16),
        ],
        scratch_shapes=[
            pltpu.VMEM((exp_local, slots, model), jnp.bfloat16),
            pltpu.VMEM((exp_local, slots, model), jnp.bfloat16),
            pltpu.VMEM((seq_count, exp_local * CAP, tok_rows), jnp.bfloat16),
            pltpu.VMEM((2 * EXPERTS, tok_rows), jnp.float32),
        ],
        compiler_params=pltpu.CompilerParams(vmem_limit_bytes=56 * 1024 * 1024),
        cost_estimate=pl.CostEstimate(
            flops=16 * exp_local * slots * model * hidden,
            bytes_accessed=12 * exp_local * model * hidden,
            transcendentals=0,
        ),
    )(x_all, w_gate, w_up, w_down)


def route_table(expert_ids, route_weights):
    tok_rows = expert_ids.shape[0]
    named = (expert_ids.T[:, None, :] == jnp.arange(EXPERTS, dtype=jnp.int32)[None, :, None])
    mask = jnp.any(named, axis=0)
    weight = jnp.sum(jnp.where(named, route_weights.T[:, None, :], 0.0), axis=0)
    before = jnp.arange(tok_rows)[:, None] < jnp.arange(tok_rows)[None, :]
    rank = jnp.dot(
        mask.astype(jnp.bfloat16), before.astype(jnp.bfloat16), preferred_element_type=jnp.float32
    )
    rank = jnp.where(mask, rank, -1.0)
    return jnp.concatenate([rank, weight], axis=0).astype(jnp.bfloat16)


def per_device(
    hidden_in,
    out_grad,
    expert_ids,
    route_weights,
    w_gate,
    w_up,
    w_down,
    query_in,
    key_in,
    value_in,
    state_before,
    grad_after,
):
    seq_count = lax.axis_size("seq")
    heads = lax.axis_size("head")
    tok_rows = expert_ids.shape[0]
    head_local = query_in.shape[1] // HD
    sent = jnp.concatenate(
        [
            hidden_in,
            out_grad.astype(jnp.bfloat16),
            route_table(expert_ids, route_weights),
        ],
        axis=1,
    )
    x_all = lax.all_gather(sent, ("seq", "head"))
    x_all = x_all.reshape(seq_count, heads, tok_rows, sent.shape[1])
    query_heads = query_in.reshape(tok_rows, head_local, HD)
    key_heads = key_in.reshape(tok_rows, head_local, HD)
    value_heads = value_in.reshape(tok_rows, head_local, HD)
    kv_local = jnp.einsum("shi,shj->hij", key_heads, value_heads, precision=HIGHEST)
    prefix = carried_in(kv_local, "seq", False) + state_before
    grad_gate, grad_up, grad_down, part = expert_call(x_all, w_gate, w_up, w_down)
    part = part.reshape(seq_count * heads, tok_rows, -1)
    moe_grad = lax.psum_scatter(part, ("seq", "head"), scatter_dimension=0, tiled=True)
    moe_grad = moe_grad.reshape(tok_rows, -1).astype(jnp.float32)
    attn_grad = (out_grad + moe_grad).reshape(tok_rows, head_local, HD)
    qd_local = jnp.einsum("thi,thj->hij", query_heads, attn_grad, precision=HIGHEST)
    suffix = carried_in(qd_local, "seq", True) + grad_after
    attn_scale = (HD * tok_rows * seq_count) ** (-0.5)
    grad_query, grad_key, grad_value = attention_backward(
        query_heads, key_heads, value_heads, attn_grad, prefix, suffix, attn_scale
    )
    return (
        grad_gate,
        grad_up,
        grad_down,
        grad_query.reshape(tok_rows, -1),
        grad_key.reshape(tok_rows, -1),
        grad_value.reshape(tok_rows, -1),
    )


def solution(mesh):
    placed = (
        P("seq", "head"),
        P("seq", "head"),
        P("seq", None),
        P("seq", None),
        P("seq", None, "head"),
        P("seq", None, "head"),
        P("seq", "head", None),
        P("seq", "head"),
        P("seq", "head"),
        P("seq", "head"),
        P("head", None, None),
        P("head", None, None),
    )
    return jax.shard_map(
        per_device,
        mesh=mesh,
        in_specs=placed,
        out_specs=(
            P("seq", None, "head"),
            P("seq", None, "head"),
            P("seq", "head", None),
            P("seq", "head"),
            P("seq", "head"),
            P("seq", "head"),
        ),
        check_vma=False,
    )
```

time: 576 us -> 328 us (0.57); the launches traced: 569 us -> 327 us
  blocking collectives: 107 us -> 0 us
  matrix products: 86.4 us -> 6.29 us
  local copies, waits for them, and re-layouts: 60 us -> 3.44 us
  Pallas kernels: 0 us -> 38.2 us
  other arithmetic: 38.1 us -> 8.12 us
  starting transfers between devices: 6.1 us -> 0.17 us
    reduce_scatter x1, waiting for transfers between devices: 0.01 us -> 140 us  [per_device(): lax.psum_scatter(part, ('seq', 'head'), scatter_dimension=0, tiled=True)]
    all_gather x4 -> x3, waiting for transfers between devices: 255 us -> 115 us  [the longest x1 84.8 us: per_device(): x_all = lax.all_gather(sent, ('seq', 'head'))]
    all_to_all x2 -> x0, blocking collectives: 107 us -> none  [the longest x1 55.4 us: per_device(): lax.all_to_all(send_rows, 'seq', split_axis=1, concat_axis=1, tiled=True)]
    dot_general x8 -> x1, matrix products: 80.2 us -> 0.14 us  [route_table(): jnp.dot(mask.astype(jnp.bfloat16), before.astype(jnp.bfloat16), preferred...]
    pallas_call x0 -> x1, Pallas kernels: none -> 38.2 us  [expert_call(): pl.pallas_call(lambda *refs: expert_kernel(seq_count, exp_local, *refs),...]
    another operation x3 -> x0, other arithmetic: 18.2 us -> none
    all_gather x2 -> x0, local copies, waits for them, and re-layouts: 17.6 us -> none  [the longest x1 9.15 us: per_device(): lax.all_gather(quarter_rows, 'head', axis=3, tiled=True)]
    gather x1 -> x0, local copies, waits for them, and re-layouts: 13.3 us -> none  [per_device(): returned.reshape(-1, model_width)[slot_dest].astype(jnp.float32)]
  transfers between devices with their start and end apart: 6 -> 4, of which waited for: 3 -> 3; matrix products, arithmetic and copies ran while one was open for 12% -> 3% of each run, Pallas kernels for 0% -> 0%
where the time goes in v1:
time: 328 us; the launch traced here: 327 us
  waiting for transfers between devices  255 us (78%)
  Pallas kernels  38.2 us (12%)
  between operations  15.7 us (5%)
  other arithmetic  8.12 us (2%)
  matrix products  6.29 us (2%)
  local copies, waits for them, and re-layouts  3.44 us (1%)
    reduce_scatter x1, waiting for transfers between devices, per_device(): lax.psum_scatter(part, ('seq', 'head'), scatter_dimension=0, tiled=True)  140 us
    all_gather x1, waiting for transfers between devices, per_device(): x_all = lax.all_gather(sent, ('seq', 'head'))  84.8 us
    pallas_call x1, Pallas kernels, expert_call(): pl.pallas_call(lambda *refs: expert_kernel(seq_count, exp_local, *refs),...  38.2 us
    all_gather x2, waiting for transfers between devices, carried_in(): lax.all_gather(shard.astype(jnp.bfloat16), axis).astype(jnp.float32)  30.6 us
  transfers between devices with their start and end apart: 4, of which 3 were waited for; matrix products, arithmetic and copies ran while one was open for 3% of the time, Pallas kernels for 0%

profile of v1, /device:TPU:0, one launch (start us, length us, event | category | flops | bytes accessed | tf_op | source)
XLA Modules:
  0.0 327.3 jit_solution(17419638861301656271)
XLA Ops:
  8.0 0.0 all-gather.7.cloned.1.call-start
  8.1 0.8 fusion.20
  8.8 0.1 fusion.8
  9.0 0.7 select_reduce_fusion
  9.7 1.0 convert_element_type.27
  10.7 1.6 maximum_maximum_fusion
  12.3 0.0 reduce-scatter.2.cloned.1.call-start
  12.4 84.8 %all-gather.7.cloned.1.call-done = bf16[4096,1152]{1,0:T(8,128)(2,1)} async-done(((bf16[128,1152]{1,0:T(8,128)(2,1)}), bf16[4096,1152]{1,0:T(8,128)(2,1)}) %all-gather.7.cloned.1.call-update) | async-done | bytes 9437200 | tf_op jit(solution)/shard_map/all_gather | solution.py:203
  97.2 38.2 %shard_map.163 = (bf16[8,2048,256]{2,1,0:T(8,128)(2,1)}, bf16[8,2048,256]{2,1,0:T(8,128)(2,1)}, bf16[8,256,2048]{2,1,0:T(8,128)(2,1)}, bf16[8,4,128,512]{3,2,1,0:T(8,128)(2,1)}) custom-call(bf16[8,4,128,1152]{3,2,1,0:T(8,128)(2,1)} %bitcast.112, bf16[8,2048,256]{2,1,0:T(8,128)(2,1)} %refs_1_.1, bf16[8,2048,256]{2,1,0:T(8,128)(2,1)} %refs_2_.1, ...), custom_call_target="tpu_custom_call" | custom-call | flops 17179869184 | bytes 50331648 | tf_op jit(solution)/shard_map/pallas_call | solution.py:138
  135.5 0.0 all-gather.9.cloned.1.call-start
  135.5 1.3 convolution_convert_fusion.1
  136.8 0.0 all-gather.11.cloned.1.call-start
  136.9 139.9 %reduce-scatter.2.cloned.1.call-done = bf16[1,128,512]{2,1,0:T(8,128)(2,1)} async-done(((bf16[32,128,512]{2,1,0:T(8,128)(2,1)}), bf16[1,128,512]{2,1,0:T(8,128)(2,1)}) %reduce-scatter.2.cloned.1.call-update) | async-done | bytes 131088 | tf_op jit(solution)/shard_map/reduce_scatter | solution.py:212
  276.8 0.9 convert_add_fusion
  277.7 0.1 copy.72
  277.9 0.4 fusion.7
  278.3 0.8 copy.61
  279.1 0.7 convolution_select_fusion
  279.8 0.0 all-gather.9.cloned.1.call-done
  279.8 1.5 fusion.1
  281.3 0.6 convolution_select_fusion.1
  281.9 0.6 convolution_bitcast_fusion.3
  282.5 0.4 fusion.6
  283.0 0.8 copy.68
  283.8 0.6 convolution_bitcast_fusion.1
  284.4 0.4 fusion.33
  284.8 30.6 %all-gather.11.cloned.1.call-done = bf16[32,128,128]{2,1,0:T(8,128)(2,1)} async-done(((bf16[4,128,128]{2,1,0:T(8,128)(2,1)}), bf16[32,128,128]{2,1,0:T(8,128)(2,1)}) %all-gather.11.cloned.1.call-update) | async-done | bytes 1048592 | tf_op jit(solution)/shard_map/all_gather | solution.py:19
  315.4 1.5 fusion
  316.9 0.7 fusion.4
  317.6 0.8 copy.69
  318.4 0.6 fusion.2
  319.0 0.8 copy.70
  (19 shorter events, 0.1 us)
Async XLA Ops:
  8.0 127.5 %copy-start = (f32[128,512]{1,0:T(8,128)S(1)}, f32[128,512]{1,0:T(8,128)}, u32[]{:S(2)}) copy-start(f32[128,512]{1,0:T(8,128)} %param.20) | copy-start | bytes 786436
  8.0 89.2 %all-gather.7.cloned.1.call-start = ((), (), s32[]{:S(2)}) async-start(), calls=%async_computation.2 | async-start | bytes 9732096 | tf_op jit(solution)/shard_map/all_gather | solution.py:203
  12.3 264.4 %reduce-scatter.2.cloned.1.call-start = ((), (), s32[]{:S(2)}) async-start(), calls=%async_computation.1 | async-start | bytes 4325376 | tf_op jit(solution)/shard_map/reduce_scatter | solution.py:212
  97.2 38.3 %copy-start.2 = (f32[128,512]{1,0:T(8,128)S(1)}, f32[128,512]{1,0:T(8,128)}, u32[]{:S(2)}) copy-start(f32[128,512]{1,0:T(8,128)} %param.21) | copy-start | bytes 786436
  97.2 179.5 %copy-start.4 = (f32[128,512]{1,0:T(8,128)S(1)}, f32[128,512]{1,0:T(8,128)}, u32[]{:S(2)}) copy-start(f32[128,512]{1,0:T(8,128)} %param.13) | copy-start | bytes 786436
  97.2 180.6 %copy-start.1 = (f32[128,512]{1,0:T(8,128)S(1)}, f32[128,512]{1,0:T(8,128)}, u32[]{:S(2)}) copy-start(f32[128,512]{1,0:T(8,128)} %param.19) | copy-start | bytes 786436
  135.4 147.1 %copy-start.5 = (f32[4,128,128]{2,1,0:T(8,128)S(1)}, f32[4,128,128]{2,1,0:T(8,128)}, u32[]{:S(2)}) copy-start(f32[4,128,128]{2,1,0:T(8,128)} %param.22) | copy-start | bytes 786436
  135.4 181.5 %copy-start.3 = (f32[4,128,128]{2,1,0:T(8,128)S(1)}, f32[4,128,128]{2,1,0:T(8,128)}, u32[]{:S(2)}) copy-start(f32[4,128,128]{2,1,0:T(8,128)} %param.23) | copy-start | bytes 786436
  135.5 144.3 %all-gather.9.cloned.1.call-start = ((), (), s32[]{:S(2)}) async-start(), calls=%async_computation.3 | async-start | bytes 1179648 | tf_op jit(solution)/shard_map/all_gather | solution.py:19
  136.8 178.6 %all-gather.11.cloned.1.call-start = ((), (), s32[]{:S(2)}) async-start(), calls=%async_computation.4 | async-start | bytes 1179648 | tf_op jit(solution)/shard_map/all_gather | solution.py:19
Sparse Core Ops, SparseCore 0:
  12.5 84.7 all-gather.6
  135.6 141.1 reduce-scatter.1
Sparse Core Ops, SparseCore 1:
  138.6 39.9 all-gather.8
  279.2 36.2 all-gather.10

commit v2 on v1

--- a/solution.py
+++ b/solution.py
@@ -12,6 +12,7 @@
 
 
 HIGHEST = lax.Precision.HIGHEST
+MESH = pl.DeviceIdType.MESH
 
 
 def carried_in(shard, axis, backward):
@@ -161,6 +162,272 @@
     )(x_all, w_gate, w_up, w_down)
 
 
+def place_of(depth):
+    s, h = lax.axis_index("seq"), lax.axis_index("head")
+    return s // 2, s % 2, h // 2, h % 2
+
+
+def device_of(z, x, y, c):
+    return (z * 2 + x, y * 2 + c)
+
+
+def partners_of(z, x, y, c):
+    other_x, other_y = 1 - x, 1 - y
+    sibling = device_of(z, x, y, 1 - c)
+    first = device_of(z, c * other_x + (1 - c) * x, (1 - c) * other_y + c * y, c)
+    second = device_of(z, (1 - c) * other_x + c * x, c * other_y + (1 - c) * y, c)
+    return sibling, first, second
+
+
+def greet(depth, z, x, y, c):
+    barrier = pltpu.get_barrier_semaphore()
+    known = list(partners_of(z, x, y, c))
+    known += [device_of((z + k) % depth, x, y, c) for k in range(1, depth)]
+    for device in known:
+        pl.semaphore_signal(barrier, inc=1, device_id=device, device_id_type=MESH)
+    pl.semaphore_wait(barrier, len(known))
+
+
+def send(source, target, send_sem, recv_sem, device):
+    copy = pltpu.make_async_remote_copy(
+        src_ref=source,
+        dst_ref=target,
+        send_sem=send_sem,
+        recv_sem=recv_sem,
+        device_id=device,
+        device_id_type=MESH,
+    )
+    copy.start()
+    return copy
+
+
+def spread_kernel(depth, own_ref, all_ref, local_sem, z_send, z_recv, p_send, p_recv):
+    z, x, y, c = place_of(depth)
+    sibling, first, second = partners_of(z, x, y, c)
+    mine_a = (1 - c) * y + c * x
+    mine_b = c * y + (1 - c) * x
+
+    def slot(zi, a, b):
+        return all_ref.at[zi, c * a + (1 - c) * b, (1 - c) * a + c * b, c]
+
+    greet(depth, z, x, y, c)
+    local = pltpu.make_async_copy(own_ref, slot(z, mine_a, mine_b), local_sem)
+    local.start()
+    along = [None] * depth
+    for k in range(1, depth):
+        along[k] = send(
+            own_ref,
+            slot(z, mine_a, mine_b),
+            z_send.at[k],
+            z_recv.at[k],
+            device_of((z + k) % depth, x, y, c),
+        )
+    sent = {}
+
+    def start(kind, k, source, target, device):
+        at = kind * depth + k
+        sent[kind, k] = send(source, target, p_send.at[at], p_recv.at[at], device)
+
+    def arrive_z(k):
+        target = slot((z + depth - k) % depth, mine_a, mine_b)
+        if k:
+            along[k].wait_recv()
+        source = target if k else own_ref
+        start(0, k, source, target, first)
+        start(1, k, source, target, second)
+        start(3, k, source, target, sibling)
+
+    def arrive_first(k):
+        sent[0, k].wait_recv()
+        target = slot((z + depth - k) % depth, 1 - mine_a, mine_b)
+        start(2, k, target, target, second)
+        start(4, k, target, target, sibling)
+
+    for t in range(depth + 1):
+        if t < depth:
+            arrive_z(t)
+        if t:
+            arrive_first(t - 1)
+    for kind, a in ((1, mine_a), (2, 1 - mine_a)):
+        for k in range(depth):
+            sent[kind, k].wait_recv()
+            target = slot((z + depth - k) % depth, a, 1 - mine_b)
+            start(kind + 4, k, target, target, sibling)
+    for kind in (3, 4, 5, 6):
+        for k in range(depth):
+            sent[kind, k].wait_recv()
+    for k in range(1, depth):
+        along[k].wait_send()
+    for copy in sent.values():
+        copy.wait_send()
+    local.wait()
+
+
+def spread(own, seq_count, heads):
+    depth = seq_count // 2
+    shape = (depth, 2, 2, 2) + own.shape
+    everything = pl.pallas_call(
+        lambda *refs: spread_kernel(depth, *refs),
+        out_shape=jax.ShapeDtypeStruct(shape, own.dtype),
+        in_specs=[pl.BlockSpec(memory_space=pl.ANY)],
+        out_specs=pl.BlockSpec(memory_space=pl.ANY),
+        scratch_shapes=[
+            pltpu.SemaphoreType.DMA,
+            pltpu.SemaphoreType.DMA((depth,)),
+            pltpu.SemaphoreType.DMA((depth,)),
+            pltpu.SemaphoreType.DMA((7 * depth,)),
+            pltpu.SemaphoreType.DMA((7 * depth,)),
+        ],
+        compiler_params=pltpu.CompilerParams(collective_id=0, has_side_effects=True),
+        cost_estimate=pl.CostEstimate(flops=0, bytes_accessed=1 << 26, transcendentals=0),
+    )(own)
+    return everything.reshape((seq_count, heads) + own.shape)
+
+
+def collect_kernel(
+    depth,
+    part_ref,
+    out_grad_ref,
+    query_ref,
+    grad_ref,
+    later_ref,
+    core_got,
+    one,
+    one_got,
+    two,
+    two_got,
+    three,
+    three_got,
+    state_out,
+    state_x,
+    pair_out,
+    pair_got,
+    send_sems,
+    recv_sems,
+    state_send,
+    state_recv,
+):
+    z, x, y, c = place_of(depth)
+    sibling, first, second = partners_of(z, x, y, c)
+    mine_a = (1 - c) * y + c * x
+    mine_b = c * y + (1 - c) * x
+    greet(depth, z, x, y, c)
+    copies = []
+    order = list(range(1, depth)) + [0]
+
+    def start(kind, k, source, target, device):
+        at = kind * depth + k
+        copy = send(source, target, send_sems.at[at], recv_sems.at[at], device)
+        copies.append(copy)
+        return copy
+
+    core, step_a, step_b, step_z = {}, {}, {}, {}
+    for k in order:
+        zi = (z + k) % depth
+        core[k] = start(0, k, part_ref.at[zi, :, :, 1 - c], core_got.at[k], sibling)
+    for k in order:
+        zi = (z + k) % depth
+        core[k].wait_recv()
+        for a in range(2):
+            for b in range(2):
+                at_x, at_y = c * a + (1 - c) * b, (1 - c) * a + c * b
+                total = part_ref[zi, at_x, at_y, c].astype(jnp.float32)
+                total = total + core_got[k, at_x, at_y].astype(jnp.float32)
+                one[k, a, b] = total.astype(jnp.bfloat16)
+        step_a[k] = start(1, k, one.at[k, 1 - mine_a], one_got.at[k], first)
+    for k in order:
+        step_a[k].wait_recv()
+        total = one[k, mine_a].astype(jnp.float32) + one_got[k].astype(jnp.float32)
+        two[k] = total.astype(jnp.bfloat16)
+        step_b[k] = start(2, k, two.at[k, 1 - mine_b], two_got.at[k], second)
+    for k in order:
+        step_b[k].wait_recv()
+        total = two[k, mine_b].astype(jnp.float32) + two_got[k].astype(jnp.float32)
+        if k:
+            three[k] = total.astype(jnp.bfloat16)
+            device = device_of((z + k) % depth, x, y, c)
+            step_z[k] = start(3, k, three.at[k], three_got.at[k], device)
+        else:
+            grad_ref[...] = out_grad_ref[...] + total
+    for k in range(1, depth):
+        step_z[k].wait_recv()
+        grad_ref[...] += three_got[k].astype(jnp.float32)
+
+    heads = later_ref.shape[0]
+    for h in range(heads):
+        cols = pl.ds(h * HD, HD)
+        later_ref[h] = lax.dot_general(
+            query_ref[:, cols],
+            grad_ref[:, cols],
+            TN,
+            precision=HIGHEST,
+            preferred_element_type=jnp.float32,
+        )
+    state_out[...] = later_ref[...].astype(jnp.bfloat16)
+    swap = send(
+        state_out,
+        state_x,
+        state_send.at[0],
+        state_recv.at[0],
+        device_of(z, 1 - x, y, c),
+    )
+    copies.append(swap)
+    swap.wait_recv()
+    got = state_x[...].astype(jnp.float32)
+    pair_out[...] = (later_ref[...] + got).astype(jnp.bfloat16)
+    shared = []
+    for k in range(1, depth):
+        device = device_of((z + k) % depth, x, y, c)
+        shared.append(
+            send(pair_out, pair_got.at[k], state_send.at[k], state_recv.at[k], device)
+        )
+    later_ref[...] = got * (1 - x).astype(jnp.float32)
+    for k in range(1, depth):
+        shared[k - 1].wait_recv()
+        counted = ((z + depth - k) % depth > z).astype(jnp.float32)
+        later_ref[...] += pair_got[k].astype(jnp.float32) * counted
+    for copy in copies + shared:
+        copy.wait_send()
+
+
+def collect(part, out_grad, query_in):
+    seq_count, heads, rows, feat = part.shape
+    depth = seq_count // 2
+    part = part.reshape(depth, 2, 2, 2, rows, feat)
+    state = (feat // HD, HD, HD)
+    kind = jnp.bfloat16
+    return pl.pallas_call(
+        lambda *refs: collect_kernel(depth, *refs),
+        out_shape=[
+            jax.ShapeDtypeStruct((rows, feat), jnp.float32),
+            jax.ShapeDtypeStruct(state, jnp.float32),
+        ],
+        in_specs=[pl.BlockSpec(memory_space=pltpu.VMEM)] * 3,
+        out_specs=[pl.BlockSpec(memory_space=pltpu.VMEM)] * 2,
+        scratch_shapes=[
+            pltpu.VMEM((depth, 2, 2, rows, feat), kind),
+            pltpu.VMEM((depth, 2, 2, rows, feat), kind),
+            pltpu.VMEM((depth, 2, rows, feat), kind),
+            pltpu.VMEM((depth, 2, rows, feat), kind),
+            pltpu.VMEM((depth, rows, feat), kind),
+            pltpu.VMEM((depth, rows, feat), kind),
+            pltpu.VMEM((depth, rows, feat), kind),
+            pltpu.VMEM(state, kind),
+            pltpu.VMEM(state, kind),
+            pltpu.VMEM(state, kind),
+            pltpu.VMEM((depth,) + state, kind),
+            pltpu.SemaphoreType.DMA((4 * depth,)),
+            pltpu.SemaphoreType.DMA((4 * depth,)),
+            pltpu.SemaphoreType.DMA((depth,)),
+            pltpu.SemaphoreType.DMA((depth,)),
+        ],
+        compiler_params=pltpu.CompilerParams(
+            collective_id=1, has_side_effects=True, vmem_limit_bytes=56 * 1024 * 1024
+        ),
+        cost_estimate=pl.CostEstimate(flops=0, bytes_accessed=1 << 26, transcendentals=0),
+    )(part, out_grad, query_in)
+
+
 def route_table(expert_ids, route_weights):
     tok_rows = expert_ids.shape[0]
     named = (expert_ids.T[:, None, :] == jnp.arange(EXPERTS, dtype=jnp.int32)[None, :, None])
@@ -200,20 +467,28 @@
         ],
         axis=1,
     )
-    x_all = lax.all_gather(sent, ("seq", "head"))
-    x_all = x_all.reshape(seq_count, heads, tok_rows, sent.shape[1])
+    if heads == 4 and seq_count % 2 == 0:
+        x_all = spread(sent, seq_count, heads)
+    else:
+        x_all = lax.all_gather(sent, ("seq", "head"))
+        x_all = x_all.reshape(seq_count, heads, tok_rows, sent.shape[1])
     query_heads = query_in.reshape(tok_rows, head_local, HD)
     key_heads = key_in.reshape(tok_rows, head_local, HD)
     value_heads = value_in.reshape(tok_rows, head_local, HD)
     kv_local = jnp.einsum("shi,shj->hij", key_heads, value_heads, precision=HIGHEST)
     prefix = carried_in(kv_local, "seq", False) + state_before
     grad_gate, grad_up, grad_down, part = expert_call(x_all, w_gate, w_up, w_down)
-    part = part.reshape(seq_count * heads, tok_rows, -1)
-    moe_grad = lax.psum_scatter(part, ("seq", "head"), scatter_dimension=0, tiled=True)
-    moe_grad = moe_grad.reshape(tok_rows, -1).astype(jnp.float32)
-    attn_grad = (out_grad + moe_grad).reshape(tok_rows, head_local, HD)
-    qd_local = jnp.einsum("thi,thj->hij", query_heads, attn_grad, precision=HIGHEST)
-    suffix = carried_in(qd_local, "seq", True) + grad_after
+    if heads == 4 and seq_count % 2 == 0:
+        attn_grad, later = collect(part, out_grad, query_in)
+        attn_grad = attn_grad.reshape(tok_rows, head_local, HD)
+        suffix = later + grad_after
+    else:
+        part = part.reshape(seq_count * heads, tok_rows, -1)
+        moe_grad = lax.psum_scatter(part, ("seq", "head"), scatter_dimension=0, tiled=True)
+        moe_grad = moe_grad.reshape(tok_rows, -1).astype(jnp.float32)
+        attn_grad = (out_grad + moe_grad).reshape(tok_rows, head_local, HD)
+        qd_local = jnp.einsum("thi,thj->hij", query_heads, attn_grad, precision=HIGHEST)
+        suffix = carried_in(qd_local, "seq", True) + grad_after
     attn_scale = (HD * tok_rows * seq_count) ** (-0.5)
     grad_query, grad_key, grad_value = attention_backward(
         query_heads, key_heads, value_heads, attn_grad, prefix, suffix, attn_scale

time: 328 us -> 190 us (0.58)
  the two profiles are of different devices: /device:TPU:0 before, /device:TPU:28 now
where the time goes in v2:
time: 190 us
  Pallas kernels  157 us (83%)
  between operations  14.2 us (7%)
  matrix products  8.73 us (5%)
  other arithmetic  5.62 us (3%)
  local copies, waits for them, and re-layouts  4.51 us (2%)
    pallas_call x1, Pallas kernels, spread(): pl.pallas_call(lambda *refs: spread_kernel(depth, *refs), out_shape=jax.S...  64.6 us
    pallas_call x1, Pallas kernels, collect(): pl.pallas_call(lambda *refs: collect_kernel(depth, *refs), out_shape=[jax...  53.7 us
    pallas_call x1, Pallas kernels, expert_call(): pl.pallas_call(lambda *refs: expert_kernel(seq_count, exp_local, *refs),...  38.2 us
  transfers between devices with their start and end apart: 1, of which 0 were waited for; matrix products, arithmetic and copies ran while one was open for 7% of the time, Pallas kernels for 83%

profile of v2, /device:TPU:28, one launch (start us, length us, event | category | flops | bytes accessed | tf_op | source)
XLA Modules:
  0.0 189.7 jit_solution(147944395172828623)
XLA Ops:
  7.2 0.0 copy-start
  7.2 0.0 all-gather.3.cloned.1.call-start
  7.2 0.9 copy-done
  8.1 2.2 %convolution_convert_fusion = bf16[4,128,128]{2,1,0:T(8,128)(2,1)} fusion(f32[128,512]{1,0:T(8,128)S(1)} %copy-done, f32[128,512]{1,0:T(8,128)} %param.21), kind=kOutput, calls=%fused_computation.14 | convolution fusion | flops 100728832 | bytes 655360 | tf_op jit(solution)/shard_map/shi,shj->hij/dot_general | solution.py:478
  10.3 0.0 all-gather.3.cloned.1.call-update
  10.4 0.7 fusion.17
  11.1 0.1 fusion.6
  11.2 0.7 select_reduce_fusion
  12.0 1.0 convert_element_type.12
  13.0 1.6 maximum_maximum_fusion.refs_0_
  14.6 64.6 %shard_map.163 = bf16[4,2,2,2,128,1152]{5,4,3,2,1,0:T(8,128)(2,1)} custom-call(bf16[128,1152]{1,0:T(8,128)(2,1)} %maximum_maximum_fusion.refs_0_), custom_call_target="tpu_custom_call" | custom-call | bytes 67108864 | tf_op jit(solution)/shard_map/pallas_call | solution.py:269
  79.2 0.0 copy-start.2
  79.2 0.0 copy-start.1
  79.3 0.0 copy-start.3
  79.3 38.2 %shard_map.164 = (bf16[8,2048,256]{2,1,0:T(8,128)(2,1)}, bf16[8,2048,256]{2,1,0:T(8,128)(2,1)}, bf16[8,256,2048]{2,1,0:T(8,128)(2,1)}, bf16[8,4,128,512]{3,2,1,0:T(8,128)(2,1)}) custom-call(bf16[8,4,128,1152]{3,2,1,0:T(8,128)(2,1)} %bitcast.86, bf16[8,2048,256]{2,1,0:T(8,128)(2,1)} %refs_1_.2, bf16[8,2048,256]{2,1,0:T(8,128)(2,1)} %refs_2_.2, ...), custom_call_target="tpu_custom_call" | custom-call | flops 17179869184 | bytes 50331648 | tf_op jit(solution)/shard_map/pallas_call | solution.py:139
  117.5 53.7 %shard_map.165 = (f32[128,512]{1,0:T(8,128)}, f32[4,128,128]{2,1,0:T(8,128)}) custom-call(bf16[4,2,2,2,128,512]{5,4,3,2,1,0:T(8,128)(2,1)} %bitcast.90, f32[128,512]{1,0:T(8,128)} %refs_1_.3, f32[128,512]{1,0:T(8,128)} %refs_2_.3), custom_call_target="tpu_custom_call" | custom-call | bytes 67108864 | tf_op jit(solution)/shard_map/pallas_call | solution.py:399
  171.2 1.1 copy.63
  172.3 0.0 copy-done.2
  172.3 0.6 convolution_select_fusion.1
  172.9 0.0 copy-done.1
  172.9 0.6 convolution_bitcast_fusion.1
  173.5 1.6 fusion.3
  175.1 0.8 copy.60
  176.0 0.7 convolution_select_fusion
  176.6 0.4 fusion.29
  177.0 1.5 fusion.1
  178.6 0.8 copy.61
  179.4 0.6 convolution_bitcast_fusion.3
  180.0 0.0 all-gather.3.cloned.1.call-done
  180.0 1.5 fusion
  181.6 0.4 fusion.5
  182.0 0.8 copy.59
  (5 shorter events, 0.0 us)
Async XLA Ops:
  7.2 1.0 copy-start
  7.2 172.9 %all-gather.3.cloned.1.call-start = ((), (), s32[]{:S(2)}) async-start(), calls=%async_computation | async-start | bytes 1179648 | tf_op jit(solution)/shard_map/all_gather | solution.py:20
  79.2 93.0 %copy-start.2 = (f32[128,512]{1,0:T(8,128)S(1)}, f32[128,512]{1,0:T(8,128)}, u32[]{:S(2)}) copy-start(f32[128,512]{1,0:T(8,128)} %param.21) | copy-start | bytes 786436
  79.2 93.6 %copy-start.1 = (f32[128,512]{1,0:T(8,128)S(1)}, f32[128,512]{1,0:T(8,128)}, u32[]{:S(2)}) copy-start(f32[128,512]{1,0:T(8,128)} %refs_2_.3) | copy-start | bytes 786436
  79.3 94.2 %copy-start.3 = (f32[4,128,128]{2,1,0:T(8,128)S(1)}, f32[4,128,128]{2,1,0:T(8,128)}, u32[]{:S(2)}) copy-start(f32[4,128,128]{2,1,0:T(8,128)} %param.23) | copy-start | bytes 786436
  117.5 64.1 %copy-start.4 = (f32[4,128,128]{2,1,0:T(8,128)S(1)}, f32[4,128,128]{2,1,0:T(8,128)}, u32[]{:S(2)}) copy-start(f32[4,128,128]{2,1,0:T(8,128)} %param.22) | copy-start | bytes 786436
Sparse Core Ops, SparseCore 0:
  10.7 56.7 all-gather.2

commit v3 on v2

--- a/solution.py
+++ b/solution.py
@@ -39,11 +39,12 @@
     return (grad_query * attn_scale, grad_key * attn_scale, grad_value * attn_scale)
 
 
+NN = (((1,), (0,)), ((), ()))
 NT = (((1,), (1,)), ((), ()))
 TN = (((0,), (0,)), ((), ()))
 
 
-def dot(a, b, dims=(((1,), (0,)), ((), ()))):
+def dot(a, b, dims=NN):
     return lax.dot_general(a, b, dims, preferred_element_type=jnp.float32)
 
 
@@ -162,6 +163,10 @@
     )(x_all, w_gate, w_up, w_down)
 
 
+def fine_dot(a, b, dims):
+    return lax.dot_general(a, b, dims, precision=HIGHEST, preferred_element_type=jnp.float32)
+
+
 def place_of(depth):
     s, h = lax.axis_index("seq"), lax.axis_index("head")
     return s // 2, s % 2, h // 2, h % 2
@@ -169,6 +174,17 @@
 
 def device_of(z, x, y, c):
     return (z * 2 + x, y * 2 + c)
+
+
+def turned(depth, z, k, back=False):
+    if depth & (depth - 1):
+        return (z + (depth - k if back else k)) % depth
+    result, bit = 0, 1
+    while bit < depth:
+        own = (z // bit) % 2
+        result = result + bit * (1 - own if k & bit else own)
+        bit *= 2
+    return result
 
 
 def partners_of(z, x, y, c):
@@ -182,7 +198,7 @@
 def greet(depth, z, x, y, c):
     barrier = pltpu.get_barrier_semaphore()
     known = list(partners_of(z, x, y, c))
-    known += [device_of((z + k) % depth, x, y, c) for k in range(1, depth)]
+    known += [device_of(turned(depth, z, k), x, y, c) for k in range(1, depth)]
     for device in known:
         pl.semaphore_signal(barrier, inc=1, device_id=device, device_id_type=MESH)
     pl.semaphore_wait(barrier, len(known))
@@ -220,7 +236,7 @@
             slot(z, mine_a, mine_b),
             z_send.at[k],
             z_recv.at[k],
-            device_of((z + k) % depth, x, y, c),
+            device_of(turned(depth, z, k), x, y, c),
         )
     sent = {}
 
@@ -229,7 +245,7 @@
         sent[kind, k] = send(source, target, p_send.at[at], p_recv.at[at], device)
 
     def arrive_z(k):
-        target = slot((z + depth - k) % depth, mine_a, mine_b)
+        target = slot(turned(depth, z, k, True), mine_a, mine_b)
         if k:
             along[k].wait_recv()
         source = target if k else own_ref
@@ -239,7 +255,7 @@
 
     def arrive_first(k):
         sent[0, k].wait_recv()
-        target = slot((z + depth - k) % depth, 1 - mine_a, mine_b)
+        target = slot(turned(depth, z, k, True), 1 - mine_a, mine_b)
         start(2, k, target, target, second)
         start(4, k, target, target, sibling)
 
@@ -251,7 +267,7 @@
     for kind, a in ((1, mine_a), (2, 1 - mine_a)):
         for k in range(depth):
             sent[kind, k].wait_recv()
-            target = slot((z + depth - k) % depth, a, 1 - mine_b)
+            target = slot(turned(depth, z, k, True), a, 1 - mine_b)
             start(kind + 4, k, target, target, sibling)
     for kind in (3, 4, 5, 6):
         for k in range(depth):
@@ -286,9 +302,17 @@
 
 def collect_kernel(
     depth,
+    attn_scale,
     part_ref,
     out_grad_ref,
     query_ref,
+    key_ref,
+    value_ref,
+    prefix_ref,
+    after_ref,
+    grad_query_ref,
+    grad_key_ref,
+    grad_value_ref,
     grad_ref,
     later_ref,
     core_got,
@@ -313,7 +337,7 @@
     mine_b = c * y + (1 - c) * x
     greet(depth, z, x, y, c)
     copies = []
-    order = list(range(1, depth)) + [0]
+    order = list(range(depth - 1, -1, -1))
 
     def start(kind, k, source, target, device):
         at = kind * depth + k
@@ -323,10 +347,10 @@
 
     core, step_a, step_b, step_z = {}, {}, {}, {}
     for k in order:
-        zi = (z + k) % depth
+        zi = turned(depth, z, k)
         core[k] = start(0, k, part_ref.at[zi, :, :, 1 - c], core_got.at[k], sibling)
     for k in order:
-        zi = (z + k) % depth
+        zi = turned(depth, z, k)
         core[k].wait_recv()
         for a in range(2):
             for b in range(2):
@@ -345,7 +369,7 @@
         total = two[k, mine_b].astype(jnp.float32) + two_got[k].astype(jnp.float32)
         if k:
             three[k] = total.astype(jnp.bfloat16)
-            device = device_of((z + k) % depth, x, y, c)
+            device = device_of(turned(depth, z, k), x, y, c)
             step_z[k] = start(3, k, three.at[k], three_got.at[k], device)
         else:
             grad_ref[...] = out_grad_ref[...] + total
@@ -354,15 +378,29 @@
         grad_ref[...] += three_got[k].astype(jnp.float32)
 
     heads = later_ref.shape[0]
+    rows = grad_ref.shape[0]
+    causal = lax.broadcasted_iota(jnp.int32, (rows, rows), 0) >= lax.broadcasted_iota(
+        jnp.int32, (rows, rows), 1
+    )
     for h in range(heads):
         cols = pl.ds(h * HD, HD)
-        later_ref[h] = lax.dot_general(
+        later_ref[h] = fine_dot(query_ref[:, cols], grad_ref[:, cols], TN)
+
+    def inside(h):
+        cols = pl.ds(h * HD, HD)
+        grad, query, key, value = (
+            grad_ref[:, cols],
             query_ref[:, cols],
-            grad_ref[:, cols],
-            TN,
-            precision=HIGHEST,
-            preferred_element_type=jnp.float32,
+            key_ref[:, cols],
+            value_ref[:, cols],
         )
+        score_grad = jnp.where(causal, fine_dot(grad, value, NT), 0.0)
+        score_match = jnp.where(causal, fine_dot(query, key, NT), 0.0)
+        grad_query = fine_dot(score_grad, key, NN) + fine_dot(grad, prefix_ref[h], NT)
+        grad_query_ref[:, cols] = grad_query * attn_scale
+        grad_key_ref[:, cols] = fine_dot(score_grad, query, TN)
+        grad_value_ref[:, cols] = fine_dot(score_match, grad, TN)
+
     state_out[...] = later_ref[...].astype(jnp.bfloat16)
     swap = send(
         state_out,
@@ -372,39 +410,48 @@
         device_of(z, 1 - x, y, c),
     )
     copies.append(swap)
+    for h in range(heads // 2):
+        inside(h)
     swap.wait_recv()
     got = state_x[...].astype(jnp.float32)
     pair_out[...] = (later_ref[...] + got).astype(jnp.bfloat16)
     shared = []
     for k in range(1, depth):
-        device = device_of((z + k) % depth, x, y, c)
+        device = device_of(turned(depth, z, k), x, y, c)
         shared.append(
             send(pair_out, pair_got.at[k], state_send.at[k], state_recv.at[k], device)
         )
-    later_ref[...] = got * (1 - x).astype(jnp.float32)
+    for h in range(heads // 2, heads):
+        inside(h)
+    later_ref[...] = after_ref[...] + got * (1 - x).astype(jnp.float32)
     for k in range(1, depth):
         shared[k - 1].wait_recv()
-        counted = ((z + depth - k) % depth > z).astype(jnp.float32)
+        counted = (turned(depth, z, k, True) > z).astype(jnp.float32)
         later_ref[...] += pair_got[k].astype(jnp.float32) * counted
+    for h in range(heads):
+        cols = pl.ds(h * HD, HD)
+        grad_key = grad_key_ref[:, cols] + fine_dot(value_ref[:, cols], later_ref[h], NT)
+        grad_key_ref[:, cols] = grad_key * attn_scale
+        grad_value = grad_value_ref[:, cols] + fine_dot(key_ref[:, cols], later_ref[h], NN)
+        grad_value_ref[:, cols] = grad_value * attn_scale
     for copy in copies + shared:
         copy.wait_send()
 
 
-def collect(part, out_grad, query_in):
+def collect(part, out_grad, query_in, key_in, value_in, prefix, after, attn_scale):
     seq_count, heads, rows, feat = part.shape
     depth = seq_count // 2
     part = part.reshape(depth, 2, 2, 2, rows, feat)
     state = (feat // HD, HD, HD)
     kind = jnp.bfloat16
     return pl.pallas_call(
-        lambda *refs: collect_kernel(depth, *refs),
-        out_shape=[
-            jax.ShapeDtypeStruct((rows, feat), jnp.float32),
-            jax.ShapeDtypeStruct(state, jnp.float32),
-        ],
-        in_specs=[pl.BlockSpec(memory_space=pltpu.VMEM)] * 3,
-        out_specs=[pl.BlockSpec(memory_space=pltpu.VMEM)] * 2,
+        lambda *refs: collect_kernel(depth, attn_scale, *refs),
+        out_shape=[jax.ShapeDtypeStruct((rows, feat), jnp.float32)] * 3,
+        in_specs=[pl.BlockSpec(memory_space=pltpu.VMEM)] * 7,
+        out_specs=[pl.BlockSpec(memory_space=pltpu.VMEM)] * 3,
         scratch_shapes=[
+            pltpu.VMEM((rows, feat), jnp.float32),
+            pltpu.VMEM(state, jnp.float32),
             pltpu.VMEM((depth, 2, 2, rows, feat), kind),
             pltpu.VMEM((depth, 2, 2, rows, feat), kind),
             pltpu.VMEM((depth, 2, rows, feat), kind),
@@ -425,7 +472,7 @@
             collective_id=1, has_side_effects=True, vmem_limit_bytes=56 * 1024 * 1024
         ),
         cost_estimate=pl.CostEstimate(flops=0, bytes_accessed=1 << 26, transcendentals=0),
-    )(part, out_grad, query_in)
+    )(part, out_grad, query_in, key_in, value_in, prefix, after)
 
 
 def route_table(expert_ids, route_weights):
@@ -478,10 +525,11 @@
     kv_local = jnp.einsum("shi,shj->hij", key_heads, value_heads, precision=HIGHEST)
     prefix = carried_in(kv_local, "seq", False) + state_before
     grad_gate, grad_up, grad_down, part = expert_call(x_all, w_gate, w_up, w_down)
+    attn_scale = (HD * tok_rows * seq_count) ** (-0.5)
     if heads == 4 and seq_count % 2 == 0:
-        attn_grad, later = collect(part, out_grad, query_in)
-        attn_grad = attn_grad.reshape(tok_rows, head_local, HD)
-        suffix = later + grad_after
+        grad_query, grad_key, grad_value = collect(
+            part, out_grad, query_in, key_in, value_in, prefix, grad_after, attn_scale
+        )
     else:
         part = part.reshape(seq_count * heads, tok_rows, -1)
         moe_grad = lax.psum_scatter(part, ("seq", "head"), scatter_dimension=0, tiled=True)
@@ -489,10 +537,9 @@
         attn_grad = (out_grad + moe_grad).reshape(tok_rows, head_local, HD)
         qd_local = jnp.einsum("thi,thj->hij", query_heads, attn_grad, precision=HIGHEST)
         suffix = carried_in(qd_local, "seq", True) + grad_after
-    attn_scale = (HD * tok_rows * seq_count) ** (-0.5)
-    grad_query, grad_key, grad_value = attention_backward(
-        query_heads, key_heads, value_heads, attn_grad, prefix, suffix, attn_scale
-    )
+        grad_query, grad_key, grad_value = attention_backward(
+            query_heads, key_heads, value_heads, attn_grad, prefix, suffix, attn_scale
+        )
     return (
         grad_gate,
         grad_up,

time: 190 us -> 184 us (0.968)
  the two profiles are of different devices: /device:TPU:28 before, /device:TPU:0 now
where the time goes in v3:
time: 184 us; the launch traced here: 183 us
  Pallas kernels  155 us (84%)
  between operations  14.1 us (8%)
  other arithmetic  6.34 us (3%)
  local copies, waits for them, and re-layouts  6.09 us (3%)
  matrix products  2.14 us (1%)
    pallas_call x1, Pallas kernels, spread(): pl.pallas_call(lambda *refs: spread_kernel(depth, *refs), out_shape=jax.S...  64.8 us
    pallas_call x1, Pallas kernels, collect(): pl.pallas_call(lambda *refs: collect_kernel(depth, attn_scale, *refs), ou...  51.6 us
    pallas_call x1, Pallas kernels, expert_call(): pl.pallas_call(lambda *refs: expert_kernel(seq_count, exp_local, *refs),...  38.2 us
    unnamed x5, local copies, waits for them, and re-layouts  5.02 us
  transfers between devices with their start and end apart: 1, of which 0 were waited for; matrix products, arithmetic and copies ran while one was open for 2% of the time, Pallas kernels for 56%

profile of v3, /device:TPU:0, one launch (start us, length us, event | category | flops | bytes accessed | tf_op | source)
XLA Modules:
  0.0 183.3 jit_solution(7176916474103004765)
XLA Ops:
  7.2 0.0 all-gather.3.cloned.1.call-start
  7.2 1.1 copy.24
  8.3 2.0 %convolution_convert_fusion = bf16[4,128,128]{2,1,0:T(8,128)(2,1)} fusion(f32[128,4,128]{0,2,1:T(8,128)S(1)} %bitcast.19, f32[128,512]{1,0:T(8,128)} %refs_4_.1), kind=kOutput, calls=%fused_computation.2 | convolution fusion | flops 100728832 | bytes 655360 | tf_op jit(solution)/shard_map/shi,shj->hij/dot_general | solution.py:525
  10.3 0.0 all-gather.3.cloned.1.call-update
  10.3 0.7 fusion.4
  11.0 0.1 fusion.1
  11.2 0.7 select_reduce_fusion
  11.9 1.0 convert_element_type.12
  12.9 1.6 maximum_maximum_fusion.refs_0_
  14.5 64.8 %shard_map.163 = bf16[4,2,2,2,128,1152]{5,4,3,2,1,0:T(8,128)(2,1)} custom-call(bf16[128,1152]{1,0:T(8,128)(2,1)} %maximum_maximum_fusion.refs_0_), custom_call_target="tpu_custom_call" | custom-call | bytes 67108864 | tf_op jit(solution)/shard_map/pallas_call | solution.py:285
  79.4 0.0 copy-start
  79.4 38.2 %shard_map.164 = (bf16[8,2048,256]{2,1,0:T(8,128)(2,1)}, bf16[8,2048,256]{2,1,0:T(8,128)(2,1)}, bf16[8,256,2048]{2,1,0:T(8,128)(2,1)}, bf16[8,4,128,512]{3,2,1,0:T(8,128)(2,1)}) custom-call(bf16[8,4,128,1152]{3,2,1,0:T(8,128)(2,1)} %bitcast.16, bf16[8,2048,256]{2,1,0:T(8,128)(2,1)} %refs_1_.2, bf16[8,2048,256]{2,1,0:T(8,128)(2,1)} %refs_2_.2, ...), custom_call_target="tpu_custom_call" | custom-call | flops 17179869184 | bytes 50331648 | tf_op jit(solution)/shard_map/pallas_call | solution.py:140
  117.6 0.0 all-gather.3.cloned.1.call-done
  117.6 1.5 fusion
  119.1 0.0 copy-done
  119.1 0.7 add.3.refs_5_
  119.9 51.6 %shard_map.165 = (f32[128,512]{1,0:T(8,128)}, f32[128,512]{1,0:T(8,128)}, f32[128,512]{1,0:T(8,128)}) custom-call(bf16[4,2,2,2,128,512]{5,4,3,2,1,0:T(8,128)(2,1)} %bitcast.17, f32[128,512]{1,0:T(8,128)} %refs_1_.3, f32[128,512]{1,0:T(8,128)} %refs_2_.3, f32[128,512]{1,0:T(8,128)} %refs_3_.3, f32[128,512]{1,0:T(8,128)} %refs_4_.1, ...), custom_call_target="tpu_custom_call" | custom-call | bytes 67108864 | tf_op jit(solution)/shard_map/pallas_call | solution.py:447
  171.4 1.7 copy.33
  173.1 1.7 copy.34
  174.8 1.7 copy.35
  (1 shorter events, 0.0 us)
Async XLA Ops:
  7.2 110.4 %all-gather.3.cloned.1.call-start = ((), (), s32[]{:S(2)}) async-start(), calls=%async_computation | async-start | bytes 1179648 | tf_op jit(solution)/shard_map/all_gather | solution.py:20
  79.4 39.8 %copy-start = (f32[4,128,128]{2,1,0:T(8,128)S(1)}, f32[4,128,128]{2,1,0:T(8,128)}, u32[]{:S(2)}) copy-start(f32[4,128,128]{2,1,0:T(8,128)} %param.22) | copy-start | bytes 786436
Sparse Core Ops, SparseCore 0:
  10.7 59.1 all-gather.2

commit v4 on v3

--- a/solution.py
+++ b/solution.py
@@ -65,13 +65,25 @@
     route,
 ):
     step = pl.program_id(0)
-    heads, tok_rows, _ = x_ref.shape
-    feat = part_ref.shape[3]
+    heads = x_ref.shape[0]
+    tok_rows, feat = part_ref.shape[2:]
+    lanes = x_ref.shape[2]
+    chunks = feat // lanes
+    share = 2 * EXPERTS // heads
+
+    def features(h, first):
+        parts = [
+            x_ref[h, (first + j) * tok_rows : (first + j + 1) * tok_rows, :]
+            for j in range(chunks)
+        ]
+        return jnp.concatenate(parts, axis=1)
 
     @pl.when(step < seq_count)
     def _gather():
         base = lax.axis_index("seq") * exp_local
-        route[...] = x_ref[0, :, 2 * feat :].astype(jnp.float32)
+        for h in range(heads):
+            table = x_ref[h, 2 * chunks * tok_rows :, :].astype(jnp.float32)
+            route[h * share : (h + 1) * share, :] = table
         ranks = lax.broadcasted_iota(jnp.int32, (CAP, tok_rows), 0).astype(jnp.float32)
         ones, scaled = [], []
         for e in range(exp_local):
@@ -86,9 +98,9 @@
         at = pl.ds(pl.multiple_of(step * CAP, CAP), CAP)
         for h in range(heads):
             cols = pl.ds(h * feat, feat)
-            got = dot(one, x_ref[h, :, :feat]).astype(jnp.bfloat16)
+            got = dot(one, features(h, 0)).astype(jnp.bfloat16)
             rows[:, at, cols] = got.reshape(exp_local, CAP, feat)
-            got = dot(weighted, x_ref[h, :, feat : 2 * feat]).astype(jnp.bfloat16)
+            got = dot(weighted, features(h, chunks)).astype(jnp.bfloat16)
             grads[:, at, cols] = got.reshape(exp_local, CAP, feat)
 
     @pl.when((step >= seq_count) & (step < seq_count + exp_local))
@@ -121,7 +133,7 @@
 
 
 def expert_call(x_all, w_gate, w_up, w_down):
-    seq_count, heads, tok_rows, width = x_all.shape
+    seq_count, heads, packed, tok_rows = x_all.shape
     exp_local, model, hidden = w_gate.shape
     feat = model // heads
     slots = seq_count * CAP
@@ -140,7 +152,7 @@
     return pl.pallas_call(
         lambda *refs: expert_kernel(seq_count, exp_local, *refs),
         grid=(2 * seq_count + exp_local,),
-        in_specs=[pl.BlockSpec((None, heads, tok_rows, width), block_in), tall, tall, flat],
+        in_specs=[pl.BlockSpec((None, heads, packed, tok_rows), block_in), tall, tall, flat],
         out_specs=[tall, tall, flat, pl.BlockSpec((1, heads, tok_rows, feat), block_out)],
         out_shape=[
             jax.ShapeDtypeStruct(w_gate.shape, jnp.bfloat16),
@@ -302,7 +314,6 @@
 
 def collect_kernel(
     depth,
-    attn_scale,
     part_ref,
     out_grad_ref,
     query_ref,
@@ -397,7 +408,7 @@
         score_grad = jnp.where(causal, fine_dot(grad, value, NT), 0.0)
         score_match = jnp.where(causal, fine_dot(query, key, NT), 0.0)
         grad_query = fine_dot(score_grad, key, NN) + fine_dot(grad, prefix_ref[h], NT)
-        grad_query_ref[:, cols] = grad_query * attn_scale
+        grad_query_ref[:, cols] = grad_query
         grad_key_ref[:, cols] = fine_dot(score_grad, query, TN)
         grad_value_ref[:, cols] = fine_dot(score_match, grad, TN)
 
@@ -431,21 +442,21 @@
     for h in range(heads):
         cols = pl.ds(h * HD, HD)
         grad_key = grad_key_ref[:, cols] + fine_dot(value_ref[:, cols], later_ref[h], NT)
-        grad_key_ref[:, cols] = grad_key * attn_scale
+        grad_key_ref[:, cols] = grad_key
         grad_value = grad_value_ref[:, cols] + fine_dot(key_ref[:, cols], later_ref[h], NN)
-        grad_value_ref[:, cols] = grad_value * attn_scale
+        grad_value_ref[:, cols] = grad_value
     for copy in copies + shared:
         copy.wait_send()
 
 
-def collect(part, out_grad, query_in, key_in, value_in, prefix, after, attn_scale):
+def collect(part, out_grad, query_in, key_in, value_in, prefix, after):
     seq_count, heads, rows, feat = part.shape
     depth = seq_count // 2
     part = part.reshape(depth, 2, 2, 2, rows, feat)
     state = (feat // HD, HD, HD)
     kind = jnp.bfloat16
     return pl.pallas_call(
-        lambda *refs: collect_kernel(depth, attn_scale, *refs),
+        lambda *refs: collect_kernel(depth, *refs),
         out_shape=[jax.ShapeDtypeStruct((rows, feat), jnp.float32)] * 3,
         in_specs=[pl.BlockSpec(memory_space=pltpu.VMEM)] * 7,
         out_specs=[pl.BlockSpec(memory_space=pltpu.VMEM)] * 3,
@@ -488,6 +499,11 @@
     return jnp.concatenate([rank, weight], axis=0).astype(jnp.bfloat16)
 
 
+def in_chunks(array):
+    rows, width = array.shape
+    return array.reshape(rows, width // rows, rows).transpose(1, 0, 2).reshape(-1, rows)
+
+
 def per_device(
     hidden_in,
     out_grad,
@@ -506,19 +522,21 @@
     heads = lax.axis_size("head")
     tok_rows = expert_ids.shape[0]
     head_local = query_in.shape[1] // HD
+    table = route_table(expert_ids, route_weights)
+    share = table.shape[0] // heads
     sent = jnp.concatenate(
         [
-            hidden_in,
-            out_grad.astype(jnp.bfloat16),
-            route_table(expert_ids, route_weights),
+            in_chunks(hidden_in),
+            in_chunks(out_grad.astype(jnp.bfloat16)),
+            lax.dynamic_slice_in_dim(table, lax.axis_index("head") * share, share, 0),
         ],
-        axis=1,
+        axis=0,
     )
     if heads == 4 and seq_count % 2 == 0:
         x_all = spread(sent, seq_count, heads)
     else:
         x_all = lax.all_gather(sent, ("seq", "head"))
-        x_all = x_all.reshape(seq_count, heads, tok_rows, sent.shape[1])
+        x_all = x_all.reshape((seq_count, heads) + sent.shape)
     query_heads = query_in.reshape(tok_rows, head_local, HD)
     key_heads = key_in.reshape(tok_rows, head_local, HD)
     value_heads = value_in.reshape(tok_rows, head_local, HD)
@@ -528,7 +546,12 @@
     attn_scale = (HD * tok_rows * seq_count) ** (-0.5)
     if heads == 4 and seq_count % 2 == 0:
         grad_query, grad_key, grad_value = collect(
-            part, out_grad, query_in, key_in, value_in, prefix, grad_after, attn_scale
+            part, out_grad, query_in, key_in, value_in, prefix, grad_after
+        )
+        grad_query, grad_key, grad_value = (
+            grad_query * attn_scale,
+            grad_key * attn_scale,
+            grad_value * attn_scale,
         )
     else:
         part = part.reshape(seq_count * heads, tok_rows, -1)

time: 184 us -> 177 us (0.962)
  Pallas kernels: 155 us -> 150 us
  local copies, waits for them, and re-layouts: 6.09 us -> 1.15 us
  other arithmetic: 6.34 us -> 9.01 us
    unnamed x5 -> x6, local copies, waits for them, and re-layouts: 5.02 us -> 0.02 us
    pallas_call x1, Pallas kernels: 64.8 us -> 60.6 us  [spread(): pl.pallas_call(lambda *refs: spread_kernel(depth, *refs), out_shape=jax.S...]
    mul x0 -> x2, other arithmetic: none -> 3.55 us  [the longest x1 1.87 us: per_device(): grad_value * attn_scale]
where the time goes in v4:
time: 177 us
  Pallas kernels  150 us (85%)
  between operations  14.1 us (8%)
  other arithmetic  9.01 us (5%)
  matrix products  2.14 us (1%)
    pallas_call x1, Pallas kernels, spread(): pl.pallas_call(lambda *refs: spread_kernel(depth, *refs), out_shape=jax.S...  60.6 us
    pallas_call x1, Pallas kernels, collect(): pl.pallas_call(lambda *refs: collect_kernel(depth, *refs), out_shape=[jax...  51.6 us
    pallas_call x1, Pallas kernels, expert_call(): pl.pallas_call(lambda *refs: expert_kernel(seq_count, exp_local, *refs),...  38.1 us
  transfers between devices with their start and end apart: 1, of which 0 were waited for; matrix products, arithmetic and copies ran while one was open for 2% of the time, Pallas kernels for 56%

profile of v4, /device:TPU:0, one launch (start us, length us, event | category | flops | bytes accessed | tf_op | source)
XLA Modules:
  0.0 176.8 jit_solution(7558205846567836499)
XLA Ops:
  7.2 0.0 copy-start
  7.2 0.0 all-gather.3.cloned.1.call-start
  7.2 1.1 copy.30
  8.3 2.0 %convolution_convert_fusion = bf16[4,128,128]{2,1,0:T(8,128)(2,1)} fusion(f32[128,4,128]{0,2,1:T(8,128)S(1)} %bitcast.35, f32[128,512]{1,0:T(8,128)} %refs_4_.1), kind=kOutput, calls=%fused_computation.2 | convolution fusion | flops 100728832 | bytes 655360 | tf_op jit(solution)/shard_map/shi,shj->hij/dot_general | solution.py:543
  10.3 0.0 all-gather.3.cloned.1.call-update
  10.4 0.7 fusion.4
  11.1 0.1 fusion.1
  11.2 0.7 select_reduce_fusion
  12.0 0.0 copy-done
  12.0 1.0 copy_bitcast_fusion
  13.0 0.7 pad_maximum_fusion.refs_0_
  13.8 60.6 %shard_map.163 = bf16[4,2,2,2,1056,128]{5,4,3,2,1,0:T(8,128)(2,1)} custom-call(bf16[1056,128]{1,0:T(8,128)(2,1)} %pad_maximum_fusion.refs_0_), custom_call_target="tpu_custom_call" | custom-call | bytes 67108864 | tf_op jit(solution)/shard_map/pallas_call | solution.py:297
  74.4 0.0 copy-start.2
  74.4 0.0 copy-start.1
  74.4 38.1 %shard_map.164 = (bf16[8,2048,256]{2,1,0:T(8,128)(2,1)}, bf16[8,2048,256]{2,1,0:T(8,128)(2,1)}, bf16[8,256,2048]{2,1,0:T(8,128)(2,1)}, bf16[8,4,128,512]{3,2,1,0:T(8,128)(2,1)}) custom-call(bf16[8,4,1056,128]{3,2,1,0:T(8,128)(2,1)} %bitcast.32, bf16[8,2048,256]{2,1,0:T(8,128)(2,1)} %refs_1_.2, bf16[8,2048,256]{2,1,0:T(8,128)(2,1)} %refs_2_.2, ...), custom_call_target="tpu_custom_call" | custom-call | flops 17179869184 | bytes 50331648 | tf_op jit(solution)/shard_map/pallas_call | solution.py:152
  112.6 0.0 all-gather.3.cloned.1.call-done
  112.6 1.5 fusion
  114.1 0.0 copy-done.2
  114.1 0.7 add.7.refs_5_
  114.8 51.6 %shard_map.165 = (f32[128,512]{1,0:T(8,128)}, f32[128,512]{1,0:T(8,128)}, f32[128,512]{1,0:T(8,128)}) custom-call(bf16[4,2,2,2,128,512]{5,4,3,2,1,0:T(8,128)(2,1)} %bitcast.33, f32[128,512]{1,0:T(8,128)} %refs_1_.3, f32[128,512]{1,0:T(8,128)} %refs_2_.3, f32[128,512]{1,0:T(8,128)} %refs_3_.3, f32[128,512]{1,0:T(8,128)} %refs_4_.1, ...), custom_call_target="tpu_custom_call" | custom-call | bytes 67108864 | tf_op jit(solution)/shard_map/pallas_call | solution.py:458
  166.4 1.7 broadcast_multiply_fusion.2
  168.1 1.9 %broadcast_multiply_fusion = (f32[128,512]{1,0:T(8,128)}, f32[128,512]{1,0:T(8,128)}) fusion(f32[128,512]{1,0:T(8,128)} %get-tuple-element.19, f32[128,512]{1,0:T(8,128)} %get-tuple-element.18), kind=kLoop, calls=%fused_computation.13 | loop fusion | flops 131072 | bytes 1048576 | tf_op jit(solution)/shard_map/mul | solution.py:554
  170.0 0.0 copy-done.1
  (3 shorter events, 0.1 us)
Async XLA Ops:
  7.2 4.8 %copy-start = (bf16[128,512]{1,0:T(8,128)(2,1)S(1)}, bf16[128,512]{1,0:T(8,128)(2,1)}, u32[]{:S(2)}) copy-start(bf16[128,512]{1,0:T(8,128)(2,1)} %param.12) | copy-start | bytes 393220
  7.2 105.4 %all-gather.3.cloned.1.call-start = ((), (), s32[]{:S(2)}) async-start(), calls=%async_computation | async-start | bytes 1179648 | tf_op jit(solution)/shard_map/all_gather | solution.py:20
  74.4 39.7 %copy-start.2 = (f32[4,128,128]{2,1,0:T(8,128)S(1)}, f32[4,128,128]{2,1,0:T(8,128)}, u32[]{:S(2)}) copy-start(f32[4,128,128]{2,1,0:T(8,128)} %param.22) | copy-start | bytes 786436
  74.4 95.6 %copy-start.1 = (bf16[128,512]{1,0:T(8,128)(2,1)S(1)}, bf16[128,512]{1,0:T(8,128)(2,1)}, u32[]{:S(2)}) copy-start(bf16[128,512]{1,0:T(8,128)(2,1)} %param.12) | copy-start | bytes 393220
Sparse Core Ops, SparseCore 0:
  10.7 57.1 all-gather.2
